TPU v7x, 32 devices: a whole 2x2x4 slice. The times are simulated.
32 devices in a mesh: job: 2 (over y), pole: 4 (over z), col: 4 (over x, core).
Axes of the slice: x: 2, y: 2, z: 4, core: 2. Of those that a mesh axis runs over, the one named last changes fastest.
Arguments:
- inverse: bfloat16 [8, 2, 6144, 6144], P(('job', 'pole'), None, 'col'), parts along dimension 0, may hold values from -6 to 6
- panels: bfloat16 [8, 3, 2, 6144, 128], P(('job', 'pole'), None, None, 'col'), parts along dimension 0, may hold values from -0.078125 to 0.078125
- diag_inverse: float32 [8, 3, 2, 128, 128], P(('job', 'pole')), parts along dimension 0, may hold values from -6 to 6
- pole_weights: float32 [8, 2], P(('job', 'pole')), parts along dimension 0, may hold values from -1 to 1
- supports: int32 [32, 8], replicated, may hold values from 0 to 143, as said below
- counts: int32 [32], replicated, may hold values from 1 to 8, as said below
- panel_order: int32 [3], replicated, may hold values from 0 to 2, each once
- row_orbitals: bfloat16 [64, 8, 128, 512], P(('job', 'col'), None, None, 'pole'), parts along dimension 0, may hold values from -0.5 to 0.5
- panel_orbitals: bfloat16 [64, 3, 128, 512], P(('job', 'col'), None, None, 'pole'), parts along dimension 0, may hold values from -0.078125 to 0.078125
- core_density: float32 [64, 512], P(('job', 'col'), 'pole'), parts along dimension 0, may hold values from 0.5 to 4
Outputs:
- valence_density: float32 [64, 512], P(('job', 'col'), 'pole'), parts along dimension 0
- exchange_potential: float32 [64, 512], P(('job', 'col'), 'pole'), parts along dimension 0
- diag_density: float32 [6, 128, 128], P('job'), parts along dimension 0
There are 2 independent parts, one for each index of `job`. A program takes and returns all parts, laid end to end along the dimension named above; an argument that names none is the same for every part. Nothing has to cross between parts.
Inputs may be any that keep to these rules, and one draw needn't show every extreme that they name: `supports`: the ids within one tile's list are distinct. Block g belongs to index g // 36 of col. Over the first counts[t] entries of all tiles of one index of col, at most 3 distinct blocks belong to any one index of col, and exactly 3 for some pair in every draw. `counts`: some tile of every index of col has a full list.
All inputs are finite; a program needn't handle non-finite values.
Results may differ from a plain program's by a relative error of at most 0.0029.
Values may be sent and summed in bfloat16 or wider, within the bound.
A program may use at most 128 MiB of HBM per device.

v0:
```python
import jax
import jax.numpy as jnp
from jax import lax
from jax.sharding import PartitionSpec as P

W = 128
PANELS = 3
S_MAX = 8
CAP = 3


exchange_coeff = (3.0 / 3.141592653589793) ** (1.0 / 3.0)
density_floor = 0.5


def body(
    inverse,
    panels,
    diag_inverse,
    pole_weights,
    supports,
    counts,
    panel_order,
    row_orbitals,
    panel_orbitals,
    core_density,
):
    rows_local = inverse.shape[2]
    order_size = inverse.shape[3]
    stacked = inverse[0].reshape(2 * rows_local, order_size)
    ordered = jnp.take(panels[0], panel_order, axis=0)
    send_rows = ordered.transpose(2, 0, 1, 3).reshape(rows_local, PANELS * 2 * W)
    product = jnp.dot(
        stacked,
        lax.all_gather(send_rows, "col", axis=0, tiled=True),
        preferred_element_type=jnp.float32,
    )
    product = product.reshape(2, rows_local, PANELS, 2, W)
    real_part = -(product[0, :, :, 0] - product[1, :, :, 1])
    imag_part = -(product[0, :, :, 1] + product[1, :, :, 0])
    weight_real = pole_weights[0, 0]
    weight_imag = pole_weights[0, 1]
    partial_density = weight_real * imag_part + weight_imag * real_part
    lower_rows = ordered.astype(jnp.float32)
    highest = lax.Precision.HIGHEST
    cross_real = jnp.einsum(
        "jiw,ijv->jwv", lower_rows[:, 0], real_part, precision=highest
    ) - jnp.einsum("jiw,ijv->jwv", lower_rows[:, 1], imag_part, precision=highest)
    cross_imag = jnp.einsum(
        "jiw,ijv->jwv", lower_rows[:, 0], imag_part, precision=highest
    ) + jnp.einsum("jiw,ijv->jwv", lower_rows[:, 1], real_part, precision=highest)
    col_index = lax.axis_index("col")
    leading = (col_index == 0).astype(jnp.float32)
    diag_ordered = jnp.take(diag_inverse[0], panel_order, axis=0)
    diag_term = leading * (weight_real * diag_ordered[:, 1] + weight_imag * diag_ordered[:, 0]) - (
        weight_real * cross_imag + weight_imag * cross_real
    )
    density_sum = lax.psum(partial_density, "pole")
    diag_density = lax.psum(diag_term, ("pole", "col"))
    density_blocks = density_sum.astype(jnp.bfloat16)
    blocks = (
        density_blocks.reshape(rows_local // W, W, PANELS, W)
        .transpose(0, 2, 1, 3)
        .reshape(-1, W, W)
    )
    per_device = blocks.shape[0]
    col_count = lax.axis_size("col")
    tile_count = row_orbitals.shape[0]
    my_supports = lax.dynamic_slice_in_dim(supports, col_index * tile_count, tile_count, 0)
    my_counts = lax.dynamic_slice_in_dim(counts, col_index * tile_count, tile_count, 0)
    live_slots = jnp.arange(S_MAX, dtype=jnp.int32)[None, :] < my_counts[:, None]
    every_live = jnp.arange(S_MAX, dtype=jnp.int32)[None, :] < counts[:, None]
    owners = supports // per_device
    local_index = supports % per_device
    mine_live = every_live & (owners == col_index)
    hit_table = (
        mine_live[:, :, None]
        & (local_index[:, :, None] == jnp.arange(per_device, dtype=jnp.int32)[None, None, :])
    ).astype(jnp.int32)
    needed = jnp.max(hit_table.reshape(col_count, tile_count * S_MAX, per_device), axis=1)
    position = jnp.cumsum(needed, axis=1) - 1
    chosen = (
        (needed[:, None, :] == 1)
        & (position[:, None, :] == jnp.arange(CAP, dtype=jnp.int32)[None, :, None])
    ).astype(jnp.bfloat16)
    outgoing = jnp.einsum(
        "dcb,bwv->dcwv", chosen, blocks, preferred_element_type=jnp.float32
    ).astype(jnp.bfloat16)
    incoming = lax.all_to_all(outgoing, "col", split_axis=0, concat_axis=0, tiled=True)
    wanted_table = (
        live_slots[:, :, None]
        & (
            my_supports[:, :, None]
            == jnp.arange(col_count * per_device, dtype=jnp.int32)[None, None, :]
        )
    ).astype(jnp.int32)
    wanted = jnp.max(wanted_table.reshape(-1, col_count * per_device), axis=0).reshape(
        col_count, per_device
    )
    slot_table = (
        jnp.cumsum(wanted, axis=1) - 1 + jnp.arange(col_count, dtype=jnp.int32)[:, None] * CAP
    ).reshape(-1)
    slot_index = jnp.where(live_slots, slot_table[my_supports], 0)
    picked = incoming.reshape(col_count * CAP, W, W)[slot_index]
    panel_pick = (
        (my_supports % PANELS)[:, :, None] == jnp.arange(PANELS, dtype=jnp.int32)[None, None, :]
    ).astype(jnp.bfloat16)
    panel_values = jnp.einsum(
        "tkj,tjmr->tkmr", panel_pick, panel_orbitals, preferred_element_type=jnp.float32
    ).astype(jnp.bfloat16)
    mixed = jnp.einsum("tkim,tkmr->tkir", picked, panel_values, preferred_element_type=jnp.float32)
    contribution = jnp.sum(row_orbitals.astype(jnp.float32) * mixed, axis=2)
    valence = jnp.sum(contribution * live_slots[:, :, None].astype(jnp.float32), axis=1)
    clamped = jnp.maximum(core_density + valence, density_floor)
    potential = -exchange_coeff * clamped ** (1.0 / 3.0)
    return (valence, potential, diag_density)


def solution(mesh):
    placed = (
        P(("job", "pole"), None, "col", None),
        P(("job", "pole"), None, None, "col", None),
        P(("job", "pole"), None, None, None, None),
        P(("job", "pole"), None),
        P(),
        P(),
        P(),
        P(("job", "col"), None, None, "pole"),
        P(("job", "col"), None, None, "pole"),
        P(("job", "col"), "pole"),
    )
    return jax.shard_map(
        body,
        mesh=mesh,
        in_specs=placed,
        out_specs=(P(("job", "col"), "pole"), P(("job", "col"), "pole"), P("job", None, None)),
        check_vma=False,
    )
```

profile of v0, /device:TPU:0, one launch (start us, length us, event | category | flops | bytes accessed | tf_op | source)
XLA Modules:
  0.0 385.8 jit_solution(12929315986518939983)
XLA Ops:
  7.2 0.8 compare_select_fusion.2
  8.0 0.7 compare_and_fusion
  8.7 0.1 copy-done
  8.9 2.3 gather_fusion
  11.2 2.8 copy.92
  14.1 0.3 fusion.57
  14.4 1.2 copy-done.5
  15.5 1.5 copy.93
  17.1 0.7 copy-done.13
  17.8 0.1 copy.89
  17.8 0.1 eq.84
  18.0 0.1 copy.88
  18.0 0.1 and.53
  18.1 0.7 convert_reduce_fusion
  18.8 0.1 copy.90
  18.9 0.8 reduce_window_sum.17
  19.7 0.1 dynamic_slice.6
  19.8 0.1 add_select_fusion
  19.9 0.1 eq.93
  20.0 0.1 fusion.51
  20.1 0.1 lt.95
  20.2 0.1 convert_reduce_fusion.1
  20.3 0.1 reshape.163
  20.4 0.2 reduce_window_sum.18
  20.6 0.1 add_add_fusion
  20.7 0.1 add.93
  20.8 0.1 reshape.174
  20.9 0.8 gather_fusion.1
  21.7 0.1 gather.18
  21.8 0.1 compare_select_fusion
  21.9 0.6 reshape.182
  22.6 1.8 gather_fusion.3
  24.4 0.7 pad_clamp_fusion
  25.1 1.3 fusion.53
  26.4 0.6 broadcast_compare_fusion
  27.0 0.7 broadcast_add_fusion
  27.7 1.5 copy_select_fusion
  29.2 2.1 convolution_convert_fusion
  31.3 2.3 broadcast_select_fusion
  33.6 50.6 %all-gather.2.cloned.1.call-done = bf16[6144,768]{0,1:T(8,128)(2,1)} async-done(((bf16[1536,768]{0,1:T(8,128)(2,1)}), bf16[6144,768]{0,1:T(8,128)(2,1)}) %all-gather.2.cloned.1.call-update) | async-done | bytes 9437200 | tf_op jit(solution)/shard_map/all_gather | solution.py:35
  84.2 37.8 %convolution_bitcast_fusion = f32[3072,768]{0,1:T(8,128)} fusion(bf16[6144,768]{0,1:T(8,128)(2,1)} %all-gather.2.cloned.1.call-done, bf16[3072,6144]{1,0:T(8,128)(2,1)} %bitcast.85), kind=kOutput, calls=%fused_computation.4 | convolution fusion | flops 28991029248 | bytes 56623104 | tf_op jit(solution)/shard_map/dot_general | solution.py:33
  122.0 13.2 %reshape.159 = f32[2,1536,3,2,128]{1,0,4,3,2:T(2,128)} reshape(f32[3072,768]{0,1:T(8,128)} %convolution_bitcast_fusion) | data formatting | bytes 18874368 | tf_op jit(solution)/shard_map/reshape | solution.py:38
  135.2 14.4 %fusion.52 = (f32[1,1536,3,1,128]{1,0,4,3,2:T(1,128)}, f32[1,1536,3,1,128]{1,0,4,3,2:T(1,128)}, f32[1,1536,3,1,128]{1,0,4,3,2:T(1,128)}, f32[1,1536,3,1,128]{1,0,4,3,2:T(1,128)}) fusion(f32[2,1536,3,2,128]{1,0,4,3,2:T(2,128)} %reshape.159), kind=kLoop, calls=%fused_computation.81 | loop fusion | bytes 18874368 | tf_op jit(solution)/shard_map/slice | solution.py:39
  149.7 5.4 %copy.111 = f32[1,1536,3,1,128]{4,1,2,3,0:T(8,128)S(1)} copy(f32[1,1536,3,1,128]{1,0,4,3,2:T(1,128)} %get-tuple-element.6) | data formatting | bytes 4718592
  155.1 6.8 %copy.112 = f32[1,1536,3,1,128]{4,1,2,3,0:T(8,128)} copy(f32[1,1536,3,1,128]{1,0,4,3,2:T(1,128)} %get-tuple-element.5) | data formatting | bytes 4718592
  161.9 4.3 %fusion = f32[3,128,128]{2,1,0:T(8,128)} fusion(bf16[3,2,1536,128]{2,3,0,1:T(8,128)(2,1)} %broadcast_select_fusion, f32[1,1536,3,1,128]{4,1,2,3,0:T(8,128)S(1)} %copy.111, f32[1,1536,3,1,128]{4,1,2,3,0:T(8,128)} %copy.112), kind=kOutput, calls=%fused_computation.6 | convolution fusion | flops 907149312 | bytes 6094848 | tf_op jit(solution)/shard_map/jiw,ijv->jwv/dot_general | solution.py:46
  166.3 2.2 fusion.2
  168.6 5.4 %copy.109 = f32[1,1536,3,1,128]{4,1,2,3,0:T(8,128)S(1)} copy(f32[1,1536,3,1,128]{1,0,4,3,2:T(1,128)} %get-tuple-element.8) | data formatting | bytes 4718592
  174.0 6.6 %copy.110 = f32[1,1536,3,1,128]{4,1,2,3,0:T(8,128)} copy(f32[1,1536,3,1,128]{1,0,4,3,2:T(1,128)} %get-tuple-element.7) | data formatting | bytes 4718592
  180.6 6.3 %fusion.4 = f32[1536,3,128]{2,0,1:T(8,128)} fusion(f32[]{:T(128)} %bitcast.9, f32[]{:T(128)} %bitcast.2, f32[1,1536,3,1,128]{4,1,2,3,0:T(8,128)S(1)} %copy.109, f32[1,1536,3,1,128]{4,1,2,3,0:T(8,128)} %copy.110, f32[1,1536,3,1,128]{4,1,2,3,0:T(8,128)} %copy-done.3, f32[1,1536,3,1,128]{4,1,2,3,0:T(8,128)} %copy.112), kind=kLoop, calls=%fused_computation.11 | loop fusion | flops 4128768 | bytes 11796488 | tf_op jit(solution)/shard_map/add | solution.py:43
  187.0 87.9 %all-reduce.4 = bf16[1536,3,128]{2,0,1:T(8,128)(2,1)S(1)} all-reduce(f32[1536,3,128]{2,0,1:T(8,128)} %fusion.4), channel_id=1, replica_groups=mesh['job'=2,'pole'=4,'col'=4] {'pole'}, use_global_device_ids=true, to_apply=%region_2.3 | all-reduce | flops 589824 | bytes 3538944 | tf_op jit(solution)/shard_map/psum | solution.py:58
  274.9 0.1 copy.98
  275.0 0.9 fusion.13
  276.0 0.8 copy.100
  276.8 3.5 all-to-all-start
  280.3 0.3 all-reduce.3.cloned.1.call-start
  280.6 4.7 %fusion.31 = f32[3,128,128]{2,1,0:T(8,128)S(1)} fusion(f32[3,128,128]{2,1,0:T(8,128)S(1)} %copy-done.12, bf16[3,2,1536,128]{2,3,0,1:T(8,128)(2,1)} %broadcast_select_fusion, f32[]{:T(128)} %bitcast.9, f32[1,1536,3,1,128]{4,1,2,3,0:T(8,128)S(1)} %copy.109, f32[1,1536,3,1,128]{4,1,2,3,0:T(8,128)} %copy.110), kind=kOutput, calls=%fused_computation.33 | convolution fusion | flops 907247616 | bytes 6291968 | tf_op jit(solution)/shard_map/jiw,ijv->jwv/dot_general | solution.py:48
  285.3 3.6 fusion.25
  288.9 2.2 gather_fusion.2
  291.1 3.8 multiply_reduce_fusion
  294.9 0.1 multiply_reduce_fusion.1
  295.1 0.6 power_multiply_fusion
  295.7 81.7 %all-reduce.3.cloned.1.call-done = f32[3,128,128]{2,1,0:T(8,128)} async-done(((f32[3,128,128]{2,1,0:T(8,128)}), f32[3,128,128]{2,1,0:T(8,128)}) %all-reduce.3.cloned.1.call-update) | async-done | bytes 196624 | tf_op jit(solution)/shard_map/psum | solution.py:59
  377.4 1.6 copy.127
  (50 shorter events, 0.4 us)
Async XLA Ops:
  7.2 1.7 copy-start
  7.2 77.0 %all-gather.2.cloned.1.call-start = ((), (), s32[]{:S(2)}) async-start(), calls=%async_computation.1 | async-start | bytes 11796480 | tf_op jit(solution)/shard_map/all_gather | solution.py:35
  8.7 5.3 %copy-start.16 = (pred[3]{0:T(512)(128)(4,1)}, pred[3]{0:T(512)(128)(4,1)S(1)}, u32[]{:S(2)}) copy-start(pred[3]{0:T(512)(128)(4,1)S(1)} %compare_and_fusion) | copy-start | bytes 13
  8.9 2.3 copy-start.15
  14.1 1.5 copy-start.5
  17.1 0.7 copy-start.13
  17.1 0.9 copy-start.19
  20.9 8.3 %copy-start.9 = (bf16[8,3,128,128]{3,2,1,0:T(8,128)(2,1)S(1)}, bf16[8,3,128,128]{3,2,1,0:T(8,128)(2,1)}, u32[]{:S(2)}) copy-start(bf16[8,3,128,128]{3,2,1,0:T(8,128)(2,1)} %param.18) | copy-start | bytes 2359300
  22.6 8.7 %copy-start.6 = (bf16[3,2,1536,128]{2,3,0,1:T(8,128)(2,1)S(1)}, bf16[3,2,1536,128]{2,3,0,1:T(8,128)(2,1)}, u32[]{:S(2)}) copy-start(bf16[3,2,1536,128]{2,3,0,1:T(8,128)(2,1)} %copy-done.5) | copy-start | bytes 7077892
  155.1 11.2 %copy-start.3 = (f32[1,1536,3,1,128]{4,1,2,3,0:T(8,128)}, f32[1,1536,3,1,128]{4,1,2,3,0:T(8,128)S(1)}, u32[]{:S(2)}) copy-start(f32[1,1536,3,1,128]{4,1,2,3,0:T(8,128)S(1)} %copy.111) | copy-start | bytes 7077892
  161.9 4.4 %copy-start.4 = (f32[1,1536,3,1,128]{4,1,2,3,0:T(8,128)S(1)}, f32[1,1536,3,1,128]{4,1,2,3,0:T(8,128)}, u32[]{:S(2)}) copy-start(f32[1,1536,3,1,128]{4,1,2,3,0:T(8,128)} %copy.112) | copy-start | bytes 7077892
  161.9 4.4 %copy-start.7 = (bf16[3,2,1536,128]{2,3,0,1:T(8,128)(2,1)S(1)}, bf16[3,2,1536,128]{2,3,0,1:T(8,128)(2,1)}, u32[]{:S(2)}) copy-start(bf16[3,2,1536,128]{2,3,0,1:T(8,128)(2,1)} %broadcast_select_fusion) | copy-start | bytes 7077892
  187.0 88.0 %copy-start.18 = (pred[4,36]{1,0:T(4,128)(4,1)S(1)}, pred[4,36]{1,0:T(4,128)(4,1)}, u32[]{:S(2)}) copy-start(pred[4,36]{1,0:T(4,128)(4,1)} %broadcast_compare_fusion) | copy-start | bytes 436
  275.0 5.5 %copy-start.12 = (f32[3,128,128]{2,1,0:T(8,128)S(1)}, f32[3,128,128]{2,1,0:T(8,128)}, u32[]{:S(2)}) copy-start(f32[3,128,128]{2,1,0:T(8,128)} %fusion) | copy-start | bytes 589828
  276.8 12.1 %all-to-all-start = ((bf16[4,3,128,128]{3,2,1,0:T(8,128)(2,1)}), bf16[4,3,128,128]{3,2,1,0:T(8,128)(2,1)S(1)}, u32[]{:S(2)}, u32[]{:S(2)}) async-start(bf16[4,3,128,128]{3,2,1,0:T(8,128)(2,1)} %copy.100), calls=%async_computation | async-start | bytes 786432 | tf_op jit(solution)/shard_map/all_to_all | solution.py:89
  280.3 5.0 %copy-start.10 = (f32[3,2,128,128]{3,2,0,1:T(8,128)S(1)}, f32[3,2,128,128]{3,2,0,1:T(8,128)}, u32[]{:S(2)}) copy-start(f32[3,2,128,128]{3,2,0,1:T(8,128)} %copy_select_fusion) | copy-start | bytes 1179652
  280.3 5.0 %copy-start.11 = (f32[3,128,128]{2,1,0:T(8,128)S(1)}, f32[3,128,128]{2,1,0:T(8,128)}, u32[]{:S(2)}) copy-start(f32[3,128,128]{2,1,0:T(8,128)} %fusion.2) | copy-start | bytes 589828
  280.3 97.1 %all-reduce.3.cloned.1.call-start = ((), (), s32[]{:S(2)}) async-start(), calls=%async_computation.2 | async-start | bytes 393216 | tf_op jit(solution)/shard_map/psum | solution.py:59
  280.6 4.8 %copy-start.2 = (f32[1,1536,3,1,128]{4,1,2,3,0:T(8,128)S(1)}, f32[1,1536,3,1,128]{4,1,2,3,0:T(8,128)}, u32[]{:S(2)}) copy-start(f32[1,1536,3,1,128]{4,1,2,3,0:T(8,128)} %copy.110) | copy-start | bytes 7077892
  280.6 4.8 %copy-start.8 = (bf16[3,2,1536,128]{2,3,0,1:T(8,128)(2,1)S(1)}, bf16[3,2,1536,128]{2,3,0,1:T(8,128)(2,1)}, u32[]{:S(2)}) copy-start(bf16[3,2,1536,128]{2,3,0,1:T(8,128)(2,1)} %broadcast_select_fusion) | copy-start | bytes 7077892
  291.1 87.9 %copy-start.1 = (bf16[1,3,2,1536,128]{4,3,2,1,0:T(8,128)(2,1)S(1)}, bf16[1,3,2,1536,128]{4,3,2,1,0:T(8,128)(2,1)}, u32[]{:S(2)}) copy-start(bf16[1,3,2,1536,128]{4,3,2,1,0:T(8,128)(2,1)} %param.11) | copy-start | bytes 7077892
  291.1 3.9 %copy-start.17 = (f32[8,128]{1,0:T(8,128)S(1)}, f32[8,128]{1,0:T(8,128)}, u32[]{:S(2)}) copy-start(f32[8,128]{1,0:T(8,128)} %param.19) | copy-start | bytes 12292
  295.0 83.9 %copy-start.14 = (f32[8,128]{1,0:T(8,128)}, f32[8,128]{1,0:T(8,128)S(1)}, u32[]{:S(2)}) copy-start(f32[8,128]{1,0:T(8,128)S(1)} %multiply_reduce_fusion.1) | copy-start | bytes 12292
Sparse Core Ops, SparseCore 0:
  17.2 66.9 all-gather.1
  289.0 88.2 all-reduce.2
where the time goes:
time: 387 us; the launch traced here: 386 us
  waiting for transfers between devices  132 us (34%)
  blocking collectives  87.9 us (23%)
  local copies, waits for them, and re-layouts  71.2 us (18%)
  matrix products  59.5 us (15%)
  other arithmetic  16.8 us (4%)
  between operations  14.3 us (4%)
    psum x1, blocking collectives, body(): density_sum = lax.psum(partial_density, 'pole')  87.9 us
    psum x1, waiting for transfers between devices, body(): diag_density = lax.psum(diag_term, ('pole', 'col'))  81.7 us
    all_gather x1, waiting for transfers between devices, body(): lax.all_gather(send_rows, 'col', axis=0, tiled=True)  50.6 us
    dot_general x1, matrix products, body(): jnp.dot(stacked, lax.all_gather(send_rows, 'col', axis=0, tiled=True), pr...  37.8 us
    unnamed x45, local copies, waits for them, and re-layouts  28 us
    slice x1, local copies, waits for them, and re-layouts, body(): real_part = -(product[0, :, :, 0] - product[1, :, :, 1])  14.4 us
    reshape x1, local copies, waits for them, and re-layouts, body(): product = product.reshape(2, rows_local, PANELS, 2, W)  13.2 us
  transfers between devices with their start and end apart: 3, of which 2 were waited for; matrix products, arithmetic and copies ran while one was open for 8% of the time, Pallas kernels for 0%

commit v1 on v0

v1 whole, which is shorter than its diff:
```python
import functools

import jax
import jax.numpy as jnp
from jax import lax
from jax.experimental import pallas as pl
from jax.experimental.pallas import tpu as pltpu
from jax.sharding import PartitionSpec as P

CAP = 3
CORES = 2
exchange_coeff = (3.0 / 3.141592653589793) ** (1.0 / 3.0)
density_floor = 0.5
MESH = pl.DeviceIdType.MESH


def pick_tile(size, options):
    for option in options:
        if size % option == 0:
            return option
    return size


def panel_kernel(
    cols,
    pieces,
    order_ref,
    chosen_ref,
    weight_ref,
    inverse_ref,
    panels_ref,
    diag_ref,
    blocks_ref,
    diag_out_ref,
    held,
    tiles,
    acc,
    dens,
    cross,
    own_sem,
    tile_sem,
    send_far,
    recv_far,
    send_mate,
    recv_mate,
):
    me = lax.axis_index("col")
    chips = cols // CORES
    my_chip, my_core = me // CORES, me % CORES
    mate = my_chip * CORES + (1 - my_core)
    panel_count, _, rows, width = panels_ref.shape
    piece = rows // pieces
    slots = tiles.shape[0]

    own_copy = pltpu.make_async_copy(panels_ref, held.at[me], own_sem)
    own_copy.start()

    def far_chip(hop):
        return (my_chip + hop) % chips

    steps = [(me, k) for k in range(pieces)]
    steps += [(mate, k) for k in range(pieces)]
    for k in range(pieces):
        for hop in range(1, chips):
            steps.append((far_chip(hop) * CORES + my_core, k))
        for hop in range(1, chips):
            steps.append((far_chip(hop) * CORES + 1 - my_core, k))

    def tile_copy(s):
        owner, k = steps[s]
        start = pl.multiple_of(owner * rows + k * piece, 128)
        return pltpu.make_async_copy(
            inverse_ref.at[:, :, pl.ds(start, piece)], tiles.at[s % slots], tile_sem.at[s % slots]
        )

    for s in range(min(slots - 1, len(steps))):
        tile_copy(s).start()

    barrier = pltpu.get_barrier_semaphore()
    pl.semaphore_signal(barrier, inc=1, device_id={"col": mate}, device_id_type=MESH)
    for hop in range(1, chips):
        pl.semaphore_signal(
            barrier, inc=1, device_id={"col": far_chip(hop) * CORES + my_core}, device_id_type=MESH
        )
    pl.semaphore_wait(barrier, chips)

    def part(ref, k):
        return ref.at[:, :, pl.ds(k * piece, piece), :]

    def far_copy(hop, k):
        return pltpu.make_async_remote_copy(
            src_ref=part(panels_ref, k),
            dst_ref=part(held.at[me], k),
            send_sem=send_far.at[hop, k],
            recv_sem=recv_far.at[hop, k],
            device_id={"col": far_chip(hop) * CORES + my_core},
            device_id_type=MESH,
        )

    def far_arrival(hop, k):
        source = (my_chip + chips - hop) % chips * CORES + my_core
        return source, pltpu.make_async_remote_copy(
            src_ref=part(panels_ref, k),
            dst_ref=part(held.at[source], k),
            send_sem=send_far.at[hop, k],
            recv_sem=recv_far.at[hop, k],
            device_id={"col": source},
            device_id_type=MESH,
        )

    def mate_copy(hop, k):
        source = (my_chip + chips - hop) % chips * CORES + my_core
        src = part(panels_ref, k) if hop == 0 else part(held.at[source], k)
        return pltpu.make_async_remote_copy(
            src_ref=src,
            dst_ref=part(held.at[source], k),
            send_sem=send_mate.at[hop, k],
            recv_sem=recv_mate.at[hop, k],
            device_id={"col": mate},
            device_id_type=MESH,
        )

    def mate_arrival(hop, k):
        source = (my_chip + chips - hop) % chips * CORES + 1 - my_core
        return pltpu.make_async_remote_copy(
            src_ref=part(panels_ref, k),
            dst_ref=part(held.at[source], k),
            send_sem=send_mate.at[hop, k],
            recv_sem=recv_mate.at[hop, k],
            device_id={"col": mate},
            device_id_type=MESH,
        )

    for k in range(pieces):
        for hop in range(1, chips):
            far_copy(hop, k).start()
    for k in range(pieces):
        mate_copy(0, k).start()
    own_copy.wait()

    tall = 2 * rows
    tile_rows = pick_tile(rows, (512, 384, 256, 128))

    far_index = [(hop, k) for k in range(pieces) for hop in range(1, chips)]
    forwarded = []

    for s in range(len(steps)):
        owner, k = steps[s]
        if s + slots - 1 < len(steps):
            tile_copy(s + slots - 1).start()
        group = 2 * (chips - 1)
        if s < pieces:
            pass
        elif s < 2 * pieces:
            mate_arrival(0, k).wait_recv()
        else:
            within = (s - 2 * pieces) % group
            if within == 0:
                for hop in range(1, chips):
                    far_arrival(chips - hop, k)[1].wait_recv()
                    mate_copy(chips - hop, k).start()
                    forwarded.append((chips - hop, k))
            if within >= chips - 1:
                mate_arrival(chips - (within - (chips - 1) + 1), k).wait_recv()
        tile_copy(s).wait()
        slot = s % slots

        def multiply(index, carry, owner=owner, k=k, slot=slot, first=(s == 0)):
            half, at = index // (rows // tile_rows), index % (rows // tile_rows)
            left = tiles[slot, half, pl.ds(at * tile_rows, tile_rows), :]
            out_rows = pl.ds(index * tile_rows, tile_rows)
            for p in range(panel_count):
                right = jnp.concatenate(
                    [held[owner, p, 0, k * piece : (k + 1) * piece, :], held[owner, p, 1, k * piece : (k + 1) * piece, :]],
                    axis=1,
                )
                term = jnp.dot(left, right, preferred_element_type=jnp.float32)
                if first:
                    acc[p, out_rows, :] = term
                else:
                    acc[p, out_rows, :] += term
            return carry

        lax.fori_loop(0, tall // tile_rows, multiply, 0)

    weight_real, weight_imag = weight_ref[0, 0], weight_ref[0, 1]
    cross[...] = jnp.zeros_like(cross)
    block_rows = rows // width

    def finish(b, carry):
        at = pl.ds(b * width, width)
        low = pl.ds(rows + b * width, width)
        for p in range(panel_count):
            top = acc[p, at, :]
            bottom = acc[p, low, :]
            real = bottom[:, width:] - top[:, :width]
            imag = -(top[:, width:] + bottom[:, :width])
            value = weight_real * imag + weight_imag * real
            other = weight_real * real - weight_imag * imag
            dens[p * block_rows + b] = value
            both = jnp.concatenate([value, other], axis=0)
            high = both.astype(jnp.bfloat16)
            rest = (both - high.astype(jnp.float32)).astype(jnp.bfloat16)
            left = jnp.concatenate([held[me, p, 0, at, :], held[me, p, 1, at, :]], axis=0)
            both = lax.dot_general(
                left,
                jnp.concatenate([high, rest], axis=1),
                (((0,), (0,)), ((), ())),
                preferred_element_type=jnp.float32,
            )
            cross[p] += both[:, :width] + both[:, width:]
        return carry

    lax.fori_loop(0, block_rows, finish, 0)
    leading = jnp.where(me == 0, 1.0, 0.0).astype(jnp.float32)
    for j in range(panel_count):
        source = order_ref[j]
        diag_out_ref[j] = (
            leading * (weight_real * diag_ref[source, 1] + weight_imag * diag_ref[source, 0]) - cross[source]
        )
    for c in range(blocks_ref.shape[0]):
        blocks_ref[c] = dens[chosen_ref[c]].astype(blocks_ref.dtype)

    for k in range(pieces):
        for hop in range(1, chips):
            far_copy(hop, k).wait_send()
        mate_copy(0, k).wait_send()
    for hop, k in forwarded:
        mate_copy(hop, k).wait_send()


def tile_kernel(ids_ref, supports_ref, counts_ref, blocks_ref, rows_ref, panels_ref, core_ref, valence_ref, potential_ref):
    tile_count, list_size = rows_ref.shape[0], rows_ref.shape[1]
    panel_count = panels_ref.shape[1]
    id_count = ids_ref.shape[0]

    def one(t, carry):
        total = jnp.zeros((1, rows_ref.shape[3]), jnp.float32)
        count = counts_ref[t]
        for k in range(list_size):
            block = supports_ref[t, k]
            place = jnp.int32(0)
            for c in range(id_count):
                place = jnp.where(ids_ref[c] == block, c, place)
            mixed = jnp.dot(
                blocks_ref[place], panels_ref[t, block % panel_count], preferred_element_type=jnp.float32
            )
            term = jnp.sum(rows_ref[t, k].astype(jnp.float32) * mixed, axis=0, keepdims=True)
            total += jnp.where(k < count, term, 0.0)
        valence_ref[pl.ds(t, 1), :] = total
        return carry

    lax.fori_loop(0, tile_count, one, 0)
    clamped = jnp.maximum(core_ref[...] + valence_ref[...], density_floor)
    potential_ref[...] = -exchange_coeff * jnp.exp(jnp.log(clamped) * (1.0 / 3.0))


def body(
    inverse,
    panels,
    diag_inverse,
    pole_weights,
    supports,
    counts,
    panel_order,
    row_orbitals,
    panel_orbitals,
    core_density,
):
    rows = inverse.shape[2]
    panel_count, width = panels.shape[1], panels.shape[4]
    cols = lax.axis_size("col")
    me = lax.axis_index("col")
    block_rows = rows // width
    per_device = block_rows * panel_count
    tile_count, list_size = row_orbitals.shape[0], row_orbitals.shape[1]
    total = cols * per_device

    all_ids = jnp.arange(total, dtype=jnp.int32)
    live = jnp.arange(list_size, dtype=jnp.int32)[None, :] < counts[:, None]
    listed = jnp.where(live, supports, -1).reshape(cols, tile_count * list_size)
    needed = jnp.any(listed[:, :, None] == all_ids[None, None, :], axis=1)
    before = (all_ids[:, None] < all_ids[None, :]) & (
        all_ids[:, None] // per_device == all_ids[None, :] // per_device
    )
    rank = jnp.sum(jnp.where(needed[:, :, None] & before[None], 1, 0), axis=1)
    slot = jnp.where(needed, all_ids[None, :] // per_device * CAP + rank, -1)
    ids = jnp.max(
        jnp.where(
            slot[:, None, :] == jnp.arange(cols * CAP, dtype=jnp.int32)[None, :, None], all_ids[None, None, :], -1
        ),
        axis=2,
    )
    mine = lax.dynamic_slice_in_dim(ids, me * CAP, CAP, 1).reshape(-1)
    local = jnp.maximum(mine - me * per_device, 0)
    column = local % panel_count
    source = jnp.zeros_like(column)
    for j in range(panel_count):
        source = jnp.where(column == j, panel_order[j], source)
    chosen = source * block_rows + local // panel_count
    my_ids = lax.dynamic_slice_in_dim(ids, me, 1, 0)[0]
    my_supports = lax.dynamic_slice_in_dim(supports, me * tile_count, tile_count, 0)
    my_counts = lax.dynamic_slice_in_dim(counts, me * tile_count, tile_count, 0)

    pieces = rows // 256 if rows % 256 == 0 else 1
    piece = rows // pieces
    chips = cols // CORES
    slots = 4
    smem = pl.BlockSpec(memory_space=pltpu.SMEM)
    vmem = pl.BlockSpec(memory_space=pltpu.VMEM)
    anywhere = pl.BlockSpec(memory_space=pl.ANY)
    blocks, diag_term = pl.pallas_call(
        functools.partial(panel_kernel, cols, pieces),
        out_shape=(
            jax.ShapeDtypeStruct((cols * CAP, width, width), jnp.float32),
            jax.ShapeDtypeStruct((panel_count, width, width), jnp.float32),
        ),
        in_specs=[smem, smem, smem, anywhere, anywhere, vmem],
        out_specs=(vmem, vmem),
        scratch_shapes=[
            pltpu.VMEM((cols, panel_count, 2, rows, width), jnp.bfloat16),
            pltpu.VMEM((slots, 2, rows, piece), jnp.bfloat16),
            pltpu.VMEM((panel_count, 2 * rows, 2 * width), jnp.float32),
            pltpu.VMEM((per_device, width, width), jnp.float32),
            pltpu.VMEM((panel_count, width, width), jnp.float32),
            pltpu.SemaphoreType.DMA,
            pltpu.SemaphoreType.DMA((slots,)),
            pltpu.SemaphoreType.DMA((chips, pieces)),
            pltpu.SemaphoreType.DMA((chips, pieces)),
            pltpu.SemaphoreType.DMA((chips, pieces)),
            pltpu.SemaphoreType.DMA((chips, pieces)),
        ],
        compiler_params=pltpu.CompilerParams(
            collective_id=0, has_side_effects=True, vmem_limit_bytes=48 * 1024 * 1024
        ),
        name="panel_products",
    )(panel_order, chosen, pole_weights, inverse[0], panels[0], diag_inverse[0])

    diag_density = lax.psum(diag_term, ("pole", "col"))
    summed = lax.psum(blocks, "pole").astype(jnp.bfloat16).reshape(cols, CAP, width, width)
    incoming = lax.all_to_all(summed, "col", split_axis=0, concat_axis=0, tiled=True)
    incoming = incoming.reshape(cols * CAP, width, width)
    valence, potential = pl.pallas_call(
        tile_kernel,
        out_shape=(
            jax.ShapeDtypeStruct(core_density.shape, jnp.float32),
            jax.ShapeDtypeStruct(core_density.shape, jnp.float32),
        ),
        in_specs=[smem, smem, smem, vmem, vmem, vmem, vmem],
        out_specs=(vmem, vmem),
        compiler_params=pltpu.CompilerParams(vmem_limit_bytes=24 * 1024 * 1024),
        name="tile_products",
    )(my_ids, my_supports, my_counts, incoming, row_orbitals, panel_orbitals, core_density)
    return (valence, potential, diag_density)


def solution(mesh):
    placed = (
        P(("job", "pole"), None, "col", None),
        P(("job", "pole"), None, None, "col", None),
        P(("job", "pole"), None, None, None, None),
        P(("job", "pole"), None),
        P(),
        P(),
        P(),
        P(("job", "col"), None, None, "pole"),
        P(("job", "col"), None, None, "pole"),
        P(("job", "col"), "pole"),
    )
    return jax.shard_map(
        body,
        mesh=mesh,
        in_specs=placed,
        out_specs=(P(("job", "col"), "pole"), P(("job", "col"), "pole"), P("job", None, None)),
        check_vma=False,
    )
```

time: 387 us -> 227 us (0.59)
  Pallas kernels: 0 us -> 68.1 us
  local copies, waits for them, and re-layouts: 71.2 us -> 8.26 us
  matrix products: 59.5 us -> 0 us
  blocking collectives: 87.9 us -> 36.6 us
  waiting for transfers between devices: 132 us -> 92.4 us
  other arithmetic: 16.8 us -> 3.38 us
    pallas_call x0 -> x2, Pallas kernels: none -> 68.1 us  [the longest x1 64.7 us: body(): pl.pallas_call(functools.partial(panel_kernel, cols, pieces), out_shape=(...]
    dot_general x8 -> x0, matrix products: 59.5 us -> none  [the longest x1 37.8 us: body(): jnp.dot(stacked, lax.all_gather(send_rows, 'col', axis=0, tiled=True), pr...]
    psum x1, blocking collectives: 87.9 us -> 36.6 us  [body(): lax.psum(blocks, 'pole').astype(jnp.bfloat16)]
    all_gather x1 -> x0, waiting for transfers between devices: 50.6 us -> none  [body(): lax.all_gather(send_rows, 'col', axis=0, tiled=True)]
    unnamed x45 -> x22, local copies, waits for them, and re-layouts: 28 us -> 5.87 us
    slice x2 -> x1, local copies, waits for them, and re-layouts: 15.8 us -> 1.36 us  [body(): source = jnp.where(column == j, panel_order[j], source)]
    reshape x2 -> x0, local copies, waits for them, and re-layouts: 13.3 us -> none  [the longest x1 13.2 us: body(): product = product.reshape(2, rows_local, PANELS, 2, W)]
    psum x1, waiting for transfers between devices: 81.7 us -> 91.7 us  [body(): diag_density = lax.psum(diag_term, ('pole', 'col'))]
  transfers between devices with their start and end apart: 3 -> 2, of which waited for: 2 -> 1; matrix products, arithmetic and copies ran while one was open for 8% -> 0% of each run, Pallas kernels for 0% -> 0%
where the time goes in v1:
time: 227 us; the launch traced here: 226 us
  waiting for transfers between devices  92.4 us (41%)
  Pallas kernels  68.1 us (30%)
  blocking collectives  36.6 us (16%)
  between operations  14.1 us (6%)
  local copies, waits for them, and re-layouts  8.26 us (4%)
  starting transfers between devices  3.5 us (2%)
  other arithmetic  3.38 us (1%)
    psum x1, waiting for transfers between devices, body(): diag_density = lax.psum(diag_term, ('pole', 'col'))  91.7 us
    pallas_call x1, Pallas kernels, body(): pl.pallas_call(functools.partial(panel_kernel, cols, pieces), out_shape=(...  64.7 us
    psum x1, blocking collectives, body(): lax.psum(blocks, 'pole').astype(jnp.bfloat16)  36.6 us
    unnamed x22, local copies, waits for them, and re-layouts  5.87 us
  transfers between devices with their start and end apart: 2, of which 1 were waited for; matrix products, arithmetic and copies ran while one was open for 0% of the time, Pallas kernels for 0%

profile of v1, /device:TPU:0, one launch (start us, length us, event | category | flops | bytes accessed | tf_op | source)
XLA Modules:
  0.0 226.3 jit_solution(14997405817584796454)
XLA Ops:
  7.2 0.7 fusion.2
  7.9 0.1 copy.21
  8.0 0.1 eq.56
  8.0 0.1 fusion
  8.2 0.1 fusion.1
  8.3 0.2 select_reduce_fusion
  8.5 0.3 select_reduce_fusion.1
  8.8 1.4 fusion.5
  10.2 0.1 copy.25
  10.2 0.1 div.38
  10.3 0.1 copy.24
  10.4 0.1 ne.83
  10.5 0.1 copy.23
  10.6 0.1 rem.50
  10.7 2.0 fusion.4.chosen_ref
  12.7 0.0 copy-start
  12.7 1.7 copy-done
  14.3 0.0 copy-start.3
  14.3 1.0 copy-done.3
  15.3 0.0 copy-start.4
  15.3 0.7 copy-done.4
  16.0 0.0 copy-start.6
  16.0 0.7 copy-done.6
  16.6 0.0 copy-start.9
  16.6 0.0 copy-start.8
  16.6 0.0 copy-start.5
  16.7 64.7 %panel_products.1 = (f32[12,128,128]{2,1,0:T(8,128)S(1)}, f32[3,128,128]{2,1,0:T(8,128)}) custom-call(s32[3]{0:T(128)S(1)} %copy-done.4, s32[12]{0:T(128)S(1)} %fusion.4.chosen_ref, f32[1,2]{1,0:T(1,128)S(1)} %copy-done.6, bf16[2,1536,6144]{2,1,0:T(8,128)(2,1)} %bitcast.11, bf16[3,2,1536,128]{3,2,1,0:T(8,128)(2,1)S(1)} %bitcast.8, ...), custom_call_target="tpu_custom_call" | custom-call | tf_op jit(solution)/shard_map/panel_products/pallas_call | solution.py:312
  81.4 0.0 copy-start.1
  81.4 36.6 %all-reduce.4 = bf16[12,128,128]{2,1,0:T(8,128)(2,1)} all-reduce(f32[12,128,128]{2,1,0:T(8,128)S(1)} %get-tuple-element.7), channel_id=1, replica_groups=mesh['job'=2,'pole'=4,'col'=4] {'pole'}, use_global_device_ids=true, to_apply=%region_3.4 | all-reduce | flops 196608 | bytes 1179648 | tf_op jit(solution)/shard_map/psum | solution.py:340
  117.9 3.5 %all-to-all-start = ((bf16[4,3,128,128]{3,2,1,0:T(8,128)(2,1)}), bf16[4,3,128,128]{3,2,1,0:T(8,128)(2,1)S(1)}, u32[]{:S(2)}, u32[]{:S(2)}) async-start(bf16[4,3,128,128]{3,2,1,0:T(8,128)(2,1)} %bitcast.6), calls=%async_computation | async-start | bytes 786432 | tf_op jit(solution)/shard_map/all_to_all | solution.py:341
  121.4 0.0 all-reduce.3.cloned.1.call-start
  121.5 0.7 all-reduce.3.cloned.1.call-update
  122.1 0.0 copy-done.9
  122.2 0.1 dynamic_slice.14.counts_ref
  122.2 0.0 copy-done.8
  122.2 0.1 constant_dynamic-slice_fusion
  122.3 0.1 copy.26.supports_ref
  122.4 0.2 dynamic-slice_reduce_fusion.ids_ref
  122.6 91.7 %all-reduce.3.cloned.1.call-done = f32[3,128,128]{2,1,0:T(8,128)} async-done(((f32[3,128,128]{2,1,0:T(8,128)}), f32[3,128,128]{2,1,0:T(8,128)}) %all-reduce.3.cloned.1.call-update) | async-done | bytes 196624 | tf_op jit(solution)/shard_map/psum | solution.py:339
  214.3 0.0 all-to-all-done
  214.3 0.0 copy-done.5
  214.3 0.0 copy-done.1
  214.3 0.0 copy-start.2
  214.3 1.1 copy-done.2
  215.5 0.0 copy-start.7
  215.5 3.3 %tile_products.1 = (f32[8,128]{1,0:T(8,128)}, f32[8,128]{1,0:T(8,128)}) custom-call(s32[12]{0:T(128)S(1)} %dynamic-slice_reduce_fusion.ids_ref, s32[8,8]{1,0:T(8,128)S(1)} %copy.26.supports_ref, s32[8]{0:T(128)S(1)} %dynamic_slice.14.counts_ref, bf16[12,128,128]{2,1,0:T(8,128)(2,1)S(1)} %bitcast.9, bf16[8,8,128,128]{3,2,1,0:T(8,128)(2,1)S(1)} %copy-done.1, ...), custom_call_target="tpu_custom_call" | custom-call | tf_op jit(solution)/shard_map/tile_products/pallas_call | solution.py:343
  218.8 0.0 copy-done.7
  218.8 0.7 copy.31
  (4 shorter events, 0.1 us)
Async XLA Ops:
  12.7 1.7 copy-start
  14.3 1.0 copy-start.3
  15.3 0.7 copy-start.4
  16.0 0.7 copy-start.6
  16.6 105.5 %copy-start.9 = (s32[32]{0:T(128)S(1)}, s32[32]{0:T(128)}, u32[]{:S(2)}) copy-start(s32[32]{0:T(128)} %param.15) | copy-start | bytes 388
  16.6 105.6 %copy-start.8 = (s32[32,8]{0,1:T(8,128)S(1)}, s32[32,8]{0,1:T(8,128)}, u32[]{:S(2)}) copy-start(s32[32,8]{0,1:T(8,128)} %param.14) | copy-start | bytes 3076
  16.6 197.7 %copy-start.5 = (f32[8,128]{1,0:T(8,128)S(1)}, f32[8,128]{1,0:T(8,128)}, u32[]{:S(2)}) copy-start(f32[8,128]{1,0:T(8,128)} %core_ref.1) | copy-start | bytes 12292
  81.4 132.9 %copy-start.1 = (bf16[8,8,128,128]{3,2,1,0:T(8,128)(2,1)S(1)}, bf16[8,8,128,128]{3,2,1,0:T(8,128)(2,1)}, u32[]{:S(2)}) copy-start(bf16[8,8,128,128]{3,2,1,0:T(8,128)(2,1)} %rows_ref.1) | copy-start | bytes 6291460
  117.9 96.4 %all-to-all-start = ((bf16[4,3,128,128]{3,2,1,0:T(8,128)(2,1)}), bf16[4,3,128,128]{3,2,1,0:T(8,128)(2,1)S(1)}, u32[]{:S(2)}, u32[]{:S(2)}) async-start(bf16[4,3,128,128]{3,2,1,0:T(8,128)(2,1)} %bitcast.6), calls=%async_computation | async-start | bytes 786432 | tf_op jit(solution)/shard_map/all_to_all | solution.py:341
  121.4 92.9 %all-reduce.3.cloned.1.call-start = ((), (), s32[]{:S(2)}) async-start(), calls=%async_computation.1 | async-start | bytes 393216 | tf_op jit(solution)/shard_map/psum | solution.py:339
  214.3 1.1 copy-start.2
  215.5 3.4 %copy-start.7 = (f32[3,128,128]{2,1,0:T(8,128)S(1)}, f32[3,128,128]{2,1,0:T(8,128)}, u32[]{:S(2)}) copy-start(f32[3,128,128]{2,1,0:T(8,128)} %all-reduce.3.cloned.1.call-done) | copy-start | bytes 589828
Sparse Core Ops, SparseCore 0:
  125.7 88.5 all-reduce.2

commit v2 on v1

--- a/solution.py
+++ b/solution.py
@@ -229,7 +229,144 @@
         mate_copy(hop, k).wait_send()
 
 
-def tile_kernel(ids_ref, supports_ref, counts_ref, blocks_ref, rows_ref, panels_ref, core_ref, valence_ref, potential_ref):
+def exchange_kernel(
+    poles,
+    cols,
+    ids_ref,
+    supports_ref,
+    counts_ref,
+    blocks_ref,
+    diag_ref,
+    rows_ref,
+    panels_ref,
+    core_ref,
+    valence_ref,
+    potential_ref,
+    diag_out_ref,
+    block_in,
+    block_sum,
+    block_full,
+    diag_in,
+    diag_col,
+    diag_full,
+    send_a,
+    recv_a,
+    send_b,
+    recv_b,
+    send_c,
+    recv_c,
+    send_d,
+    recv_d,
+    send_e,
+    recv_e,
+    send_f,
+    recv_f,
+):
+    pole, col = lax.axis_index("pole"), lax.axis_index("col")
+    part = blocks_ref.shape[1] // poles
+
+    barrier = pltpu.get_barrier_semaphore()
+    for hop in range(1, poles):
+        pl.semaphore_signal(barrier, inc=1, device_id={"pole": (pole + hop) % poles}, device_id_type=MESH)
+    for hop in range(1, cols):
+        pl.semaphore_signal(barrier, inc=1, device_id={"col": (col + hop) % cols}, device_id_type=MESH)
+    pl.semaphore_wait(barrier, poles + cols - 2)
+
+    def slice_of(index):
+        return pl.ds(pl.multiple_of(index * part, part), part)
+
+    def to_pole(src, dst, hop, send, recv):
+        return pltpu.make_async_remote_copy(
+            src_ref=src,
+            dst_ref=dst,
+            send_sem=send,
+            recv_sem=recv,
+            device_id={"pole": (pole + hop) % poles},
+            device_id_type=MESH,
+        )
+
+    def to_col(src, dst, hop, send, recv):
+        return pltpu.make_async_remote_copy(
+            src_ref=src,
+            dst_ref=dst,
+            send_sem=send,
+            recv_sem=recv,
+            device_id={"col": (col + hop) % cols},
+            device_id_type=MESH,
+        )
+
+    hops = sorted(range(1, poles), key=lambda h: -min(h, poles - h))
+    first, first_diag = {}, {}
+    for hop in hops:
+        there = slice_of((pole + hop) % poles)
+        first[hop] = to_pole(blocks_ref.at[:, there, :], block_in.at[hop], hop, send_a.at[hop], recv_a.at[hop])
+        first[hop].start()
+    for hop in hops:
+        there = slice_of((pole + hop) % poles)
+        first_diag[hop] = to_pole(diag_ref.at[:, there, :], diag_in.at[hop], hop, send_d.at[hop], recv_d.at[hop])
+        first_diag[hop].start()
+
+    here = slice_of(pole)
+    total = blocks_ref[:, here, :].astype(jnp.float32)
+    for hop in hops:
+        first[hop].wait_recv()
+        total += block_in[hop].astype(jnp.float32)
+    block_sum[...] = total.astype(block_sum.dtype)
+    second = {}
+    for hop in range(1, cols):
+        dest = (col + hop) % cols
+        second[hop] = to_col(
+            block_sum.at[pl.ds(dest * CAP, CAP)],
+            block_full.at[pl.ds(col * CAP, CAP), here, :],
+            hop,
+            send_b.at[hop],
+            recv_b.at[hop],
+        )
+        second[hop].start()
+    mine = pl.ds(col * CAP, CAP)
+    block_full[mine, here, :] = block_sum[mine]
+
+    third = []
+
+    def spread(back):
+        source = (col + cols - back) % cols
+        view = block_full.at[pl.ds(source * CAP, CAP), here, :]
+        for hop in hops:
+            copy = to_pole(view, view, hop, send_c.at[hop, back], recv_c.at[hop, back])
+            copy.start()
+            third.append(copy)
+
+    spread(0)
+    diag_total = diag_ref[:, here, :]
+    for hop in hops:
+        first_diag[hop].wait_recv()
+        diag_total += diag_in[hop]
+    diag_col[col] = diag_total
+    second_diag = {}
+    for hop in range(1, cols):
+        second_diag[hop] = to_col(
+            diag_col.at[col], diag_col.at[col], hop, send_e.at[hop], recv_e.at[hop]
+        )
+    for hop in range(1, cols):
+        second[hop].wait_recv()
+        spread(hop)
+    for hop in range(1, cols):
+        second_diag[hop].start()
+    for hop in range(1, cols):
+        second_diag[hop].wait_recv()
+    diag_total = diag_col[0]
+    for c in range(1, cols):
+        diag_total += diag_col[c]
+    diag_full[:, here, :] = diag_total
+    third_diag = []
+    for hop in hops:
+        view = diag_full.at[:, here, :]
+        copy = to_pole(view, view, hop, send_f.at[hop], recv_f.at[hop])
+        copy.start()
+        third_diag.append(copy)
+    for copy in third:
+        copy.wait_recv()
+
     tile_count, list_size = rows_ref.shape[0], rows_ref.shape[1]
     panel_count = panels_ref.shape[1]
     id_count = ids_ref.shape[0]
@@ -243,7 +380,7 @@
             for c in range(id_count):
                 place = jnp.where(ids_ref[c] == block, c, place)
             mixed = jnp.dot(
-                blocks_ref[place], panels_ref[t, block % panel_count], preferred_element_type=jnp.float32
+                block_full[place], panels_ref[t, block % panel_count], preferred_element_type=jnp.float32
             )
             term = jnp.sum(rows_ref[t, k].astype(jnp.float32) * mixed, axis=0, keepdims=True)
             total += jnp.where(k < count, term, 0.0)
@@ -253,6 +390,15 @@
     lax.fori_loop(0, tile_count, one, 0)
     clamped = jnp.maximum(core_ref[...] + valence_ref[...], density_floor)
     potential_ref[...] = -exchange_coeff * jnp.exp(jnp.log(clamped) * (1.0 / 3.0))
+
+    for copy in third_diag:
+        copy.wait_recv()
+    diag_out_ref[...] = diag_full[...]
+    for group in (first, first_diag, second, second_diag):
+        for copy in group.values():
+            copy.wait_send()
+    for copy in third + third_diag:
+        copy.wait_send()
 
 
 def body(
@@ -312,7 +458,7 @@
     blocks, diag_term = pl.pallas_call(
         functools.partial(panel_kernel, cols, pieces),
         out_shape=(
-            jax.ShapeDtypeStruct((cols * CAP, width, width), jnp.float32),
+            jax.ShapeDtypeStruct((cols * CAP, width, width), jnp.bfloat16),
             jax.ShapeDtypeStruct((panel_count, width, width), jnp.float32),
         ),
         in_specs=[smem, smem, smem, anywhere, anywhere, vmem],
@@ -336,21 +482,44 @@
         name="panel_products",
     )(panel_order, chosen, pole_weights, inverse[0], panels[0], diag_inverse[0])
 
-    diag_density = lax.psum(diag_term, ("pole", "col"))
-    summed = lax.psum(blocks, "pole").astype(jnp.bfloat16).reshape(cols, CAP, width, width)
-    incoming = lax.all_to_all(summed, "col", split_axis=0, concat_axis=0, tiled=True)
-    incoming = incoming.reshape(cols * CAP, width, width)
-    valence, potential = pl.pallas_call(
-        tile_kernel,
+    poles = lax.axis_size("pole")
+    part = width // poles
+    chosen_count = cols * CAP
+    dma = pltpu.SemaphoreType.DMA
+    valence, potential, diag_density = pl.pallas_call(
+        functools.partial(exchange_kernel, poles, cols),
         out_shape=(
             jax.ShapeDtypeStruct(core_density.shape, jnp.float32),
             jax.ShapeDtypeStruct(core_density.shape, jnp.float32),
+            jax.ShapeDtypeStruct(diag_term.shape, jnp.float32),
         ),
-        in_specs=[smem, smem, smem, vmem, vmem, vmem, vmem],
-        out_specs=(vmem, vmem),
-        compiler_params=pltpu.CompilerParams(vmem_limit_bytes=24 * 1024 * 1024),
-        name="tile_products",
-    )(my_ids, my_supports, my_counts, incoming, row_orbitals, panel_orbitals, core_density)
+        in_specs=[smem, smem, smem, vmem, vmem, vmem, vmem, vmem],
+        out_specs=(vmem, vmem, vmem),
+        scratch_shapes=[
+            pltpu.VMEM((poles, chosen_count, part, width), jnp.bfloat16),
+            pltpu.VMEM((chosen_count, part, width), jnp.bfloat16),
+            pltpu.VMEM((chosen_count, width, width), jnp.bfloat16),
+            pltpu.VMEM((poles, panel_count, part, width), jnp.float32),
+            pltpu.VMEM((cols, panel_count, part, width), jnp.float32),
+            pltpu.VMEM((panel_count, width, width), jnp.float32),
+            dma((poles,)),
+            dma((poles,)),
+            dma((cols,)),
+            dma((cols,)),
+            dma((poles, cols)),
+            dma((poles, cols)),
+            dma((poles,)),
+            dma((poles,)),
+            dma((cols,)),
+            dma((cols,)),
+            dma((poles,)),
+            dma((poles,)),
+        ],
+        compiler_params=pltpu.CompilerParams(
+            collective_id=1, has_side_effects=True, vmem_limit_bytes=24 * 1024 * 1024
+        ),
+        name="block_exchange",
+    )(my_ids, my_supports, my_counts, blocks, diag_term, row_orbitals, panel_orbitals, core_density)
     return (valence, potential, diag_density)
 
 

time: 227 us -> 110 us (0.48)
  waiting for transfers between devices: 92.4 us -> 0 us
  blocking collectives: 36.6 us -> 0 us
  Pallas kernels: 68.1 us -> 95.4 us
  between operations: 14.1 us -> 0.74 us
  starting transfers between devices: 3.5 us -> 0 us
    psum x1 -> x0, waiting for transfers between devices: 91.7 us -> none  [body(): diag_density = lax.psum(diag_term, ('pole', 'col'))]
    psum x1 -> x0, blocking collectives: 36.6 us -> none  [body(): lax.psum(blocks, 'pole').astype(jnp.bfloat16)]
    pallas_call x1, Pallas kernels: 3.35 us -> 31.4 us  [body(): pl.pallas_call(functools.partial(exchange_kernel, poles, cols), out_shape...]
    all_to_all x1 -> x0, starting transfers between devices: 3.46 us -> none  [body(): lax.all_to_all(summed, 'col', split_axis=0, concat_axis=0, tiled=True)]
    unnamed x22 -> x18, local copies, waits for them, and re-layouts: 5.87 us -> 5.91 us
  transfers between devices with their start and end apart: 2 -> 0, of which waited for: 1 -> 0; matrix products, arithmetic and copies ran while one was open for 0% -> 0% of each run, Pallas kernels for 0% -> 0%
where the time goes in v2:
time: 110 us; the launch traced here: 109 us
  Pallas kernels  95.4 us (87%)
  local copies, waits for them, and re-layouts  9.66 us (9%)
  other arithmetic  3.37 us (3%)
    pallas_call x1, Pallas kernels, body(): pl.pallas_call(functools.partial(panel_kernel, cols, pieces), out_shape=(...  64 us
    pallas_call x1, Pallas kernels, body(): pl.pallas_call(functools.partial(exchange_kernel, poles, cols), out_shape...  31.4 us
    unnamed x18, local copies, waits for them, and re-layouts  5.91 us

profile of v2, /device:TPU:0, one launch (start us, length us, event | category | flops | bytes accessed | tf_op | source)
XLA Modules:
  0.0 109.2 jit_solution(14294125769633868404)
XLA Ops:
  0.6 0.7 dynamic_slice.14.counts_ref
  1.4 1.4 %fusion.5 = (s32[1]{0:T(128)}, s32[1]{0:T(128)}, s32[1]{0:T(128)}) fusion(s32[3]{0:T(128)} %order_ref.1), kind=kLoop, calls=%fused_computation.28 | loop fusion | bytes 24 | tf_op jit(solution)/shard_map/slice | solution.py:445
  2.7 0.8 constant_dynamic-slice_fusion
  3.5 0.1 copy.26.supports_ref
  3.6 0.7 fusion.2
  4.3 0.1 copy.21
  4.3 0.1 eq.56
  4.4 0.1 fusion
  4.6 0.1 fusion.1
  4.7 0.2 select_reduce_fusion
  4.8 0.3 select_reduce_fusion.1
  5.1 0.2 dynamic-slice_reduce_fusion.ids_ref
  5.4 0.1 copy.25
  5.5 0.1 div.38
  5.5 0.1 copy.24
  5.6 0.1 ne.83
  5.7 0.1 copy.23
  5.8 0.1 rem.50
  5.9 2.0 %fusion.4.chosen_ref = s32[12]{0:T(128)S(1)} fusion(s32[12]{0:T(128)S(1)} %rem.50, s32[12]{0:T(128)S(1)} %div.38, pred[12]{0:T(512)(128)(4,1)S(1)} %ne.83, s32[]{:T(128)} %bitcast.2, s32[]{:T(128)} %bitcast.1, s32[]{:T(128)} %bitcast), kind=kLoop, calls=%fused_computation.26 | loop fusion | flops 192 | bytes 168 | tf_op jit(solution)/shard_map/add | solution.py:446
  7.9 0.0 copy-start
  7.9 1.7 %copy-done = bf16[1,3,2,1536,128]{4,3,2,1,0:T(8,128)(2,1)S(1)} copy-done((bf16[1,3,2,1536,128]{4,3,2,1,0:T(8,128)(2,1)S(1)}, bf16[1,3,2,1536,128]{4,3,2,1,0:T(8,128)(2,1)}, u32[]{:S(2)}) %copy-start) | copy-done | bytes 2359320
  9.5 0.0 copy-start.3
  9.5 1.0 copy-done.3
  10.5 0.0 copy-start.4
  10.5 0.7 copy-done.4
  11.2 0.0 copy-start.6
  11.2 0.7 copy-done.6
  11.8 0.0 copy-start.1
  11.9 0.0 copy-start.2
  11.9 0.0 copy-start.5
  11.9 64.0 %panel_products.1 = (bf16[12,128,128]{2,1,0:T(8,128)(2,1)S(1)}, f32[3,128,128]{2,1,0:T(8,128)S(1)}) custom-call(s32[3]{0:T(128)S(1)} %copy-done.4, s32[12]{0:T(128)S(1)} %fusion.4.chosen_ref, f32[1,2]{1,0:T(1,128)S(1)} %copy-done.6, bf16[2,1536,6144]{2,1,0:T(8,128)(2,1)} %bitcast.8, bf16[3,2,1536,128]{3,2,1,0:T(8,128)(2,1)S(1)} %bitcast.6, ...), custom_call_target="tpu_custom_call" | custom-call | tf_op jit(solution)/shard_map/panel_products/pallas_call | solution.py:458
  75.9 0.0 copy-done.1
  75.9 0.0 copy-done.2
  75.9 0.0 copy-done.5
  75.9 31.4 %block_exchange.1 = (f32[8,128]{1,0:T(8,128)S(1)}, f32[8,128]{1,0:T(8,128)S(1)}, f32[3,128,128]{2,1,0:T(8,128)S(1)}) custom-call(s32[12]{0:T(128)S(1)} %dynamic-slice_reduce_fusion.ids_ref, s32[8,8]{1,0:T(8,128)S(1)} %copy.26.supports_ref, s32[8]{0:T(128)S(1)} %dynamic_slice.14.counts_ref, bf16[12,128,128]{2,1,0:T(8,128)(2,1)S(1)} %get-tuple-element.5.blocks_ref, ...), custom_call_target="tpu_custom_call" | custom-call | tf_op jit(solution)/shard_map/block_exchange/pallas_call | solution.py:489
  107.3 0.6 copy.30
  107.9 0.6 copy.31
  108.5 0.7 copy.32
  (4 shorter events, 0.1 us)
Async XLA Ops:
  7.9 1.7 %copy-start = (bf16[1,3,2,1536,128]{4,3,2,1,0:T(8,128)(2,1)S(1)}, bf16[1,3,2,1536,128]{4,3,2,1,0:T(8,128)(2,1)}, u32[]{:S(2)}) copy-start(bf16[1,3,2,1536,128]{4,3,2,1,0:T(8,128)(2,1)} %param.11) | copy-start | bytes 7077892
  9.5 1.0 copy-start.3
  10.5 0.7 copy-start.4
  11.2 0.7 copy-start.6
  11.8 64.0 %copy-start.1 = (bf16[8,8,128,128]{3,2,1,0:T(8,128)(2,1)S(1)}, bf16[8,8,128,128]{3,2,1,0:T(8,128)(2,1)}, u32[]{:S(2)}) copy-start(bf16[8,8,128,128]{3,2,1,0:T(8,128)(2,1)} %rows_ref.1) | copy-start | bytes 6291460
  11.9 64.1 %copy-start.2 = (bf16[8,3,128,128]{3,2,1,0:T(8,128)(2,1)S(1)}, bf16[8,3,128,128]{3,2,1,0:T(8,128)(2,1)}, u32[]{:S(2)}) copy-start(bf16[8,3,128,128]{3,2,1,0:T(8,128)(2,1)} %panels_ref.1) | copy-start | bytes 2359300
  11.9 64.1 %copy-start.5 = (f32[8,128]{1,0:T(8,128)S(1)}, f32[8,128]{1,0:T(8,128)}, u32[]{:S(2)}) copy-start(f32[8,128]{1,0:T(8,128)} %core_ref.1) | copy-start | bytes 12292
